TPU v7x, 256 devices: a whole 4x4x8 slice. The times are simulated.
256 devices in a mesh: leaf: 64 (over z, y, core), rhs: 4 (over x).
Axes of the slice: x: 4, y: 4, z: 8, core: 2. Of those that a mesh axis runs over, the one named last changes fastest.
Arguments:
- targets: float32 [16, 524288], P('rhs', 'leaf'), may hold values from -6 to 6
- points: float32 [8, 524288], P(None, 'leaf'), may hold values from -5 to 5
- tree_order: int32 [524288], P('leaf'), may hold values from 0 to 8191, as said below
- leaf_basis: bfloat16 [2048, 256, 128], P('leaf'), may hold values from -0.375 to 0.375
- transfer_local: bfloat16 [1984, 256, 128], P('leaf'), may hold values from -0.375 to 0.375
- coupling_local: bfloat16 [1984, 128, 128], P('leaf'), may hold values from -0.25 to 0.25
- transfer_top: bfloat16 [63, 256, 128], P(None, None, 'rhs'), may hold values from -0.375 to 0.375
- coupling_top: bfloat16 [63, 128, 128], P(None, None, 'rhs'), may hold values from -0.25 to 0.25
Outputs:
- solution_out: float32 [16, 524288], P('rhs', 'leaf')
- residual_out: float32 [16, 524288], P('rhs', 'leaf')
Inputs may be any that keep to these rules, and one draw needn't show every extreme that they name: `tree_order`: each aligned block of 8192 entries is a permutation of 0 to 8191.
All inputs are finite; a program needn't handle non-finite values.
Results may differ from a plain program's by a relative error of at most 0.011.
Values may be sent and summed in bfloat16 or wider, within the bound.
A program may use at most 128 MiB of HBM per device.

v0:
```python
import jax
import jax.numpy as jnp
from jax import lax
from jax.sharding import PartitionSpec as P

LEAF = 256
ITERS = 2


exact_mode = lax.Precision.HIGHEST
kernel_rate = 0.0625
ridge_term = 1.0


def from_partner(shard, axis, stride):
    return lax.ppermute(shard, axis, [(i, i ^ 1 << stride) for i in range(lax.axis_size(axis))])


def kernel_block(pts_tree, vector):
    columns = vector.shape[0]
    width = LEAF
    blocks = vector.shape[1] // width
    spots = pts_tree.reshape(pts_tree.shape[0], blocks, width)
    distance = jnp.zeros((blocks, width, width), jnp.float32)
    for feature in range(pts_tree.shape[0]):
        spread = spots[feature, :, :, None] - spots[feature, :, None, :]
        distance = distance + spread * spread
    kernel = jnp.exp(-kernel_rate * distance)
    values = vector.reshape(columns, blocks, width)
    result = jnp.einsum(
        "cla,lab->clb", values, kernel, precision=exact_mode, preferred_element_type=jnp.float32
    )
    return (result + ridge_term * values).reshape(columns, -1)


def climb(coeffs, transfer):
    number, columns, rank = coeffs.shape
    saved = []
    offset = 0
    while number > 1:
        halves = number // 2
        paired = coeffs.reshape(halves, 2, columns, rank)
        joined = jnp.concatenate([paired[:, 0], paired[:, 1]], axis=-1)
        coeffs = jnp.einsum(
            "hcq,hqr->hcr",
            joined,
            transfer[offset : offset + halves],
            preferred_element_type=jnp.float32,
        ).astype(jnp.bfloat16)
        saved.append((paired, offset, halves))
        offset += halves
        number = halves
    return (coeffs, saved)


def descend(root_field, saved, transfer, coupling):
    columns, rank = root_field.shape
    field = root_field[None]
    for paired, offset, halves in reversed(saved):
        matrices = transfer[offset : offset + halves].reshape(halves, 2, rank, rank)
        links = coupling[offset : offset + halves]
        child = jnp.einsum(
            "hcb,hsab->hsca",
            field.astype(jnp.bfloat16),
            matrices,
            preferred_element_type=jnp.float32,
        )
        toward_left = jnp.einsum(
            "hcb,hab->hca", paired[:, 1], links, preferred_element_type=jnp.float32
        )
        toward_right = jnp.einsum(
            "hca,hab->hcb", paired[:, 0], links, preferred_element_type=jnp.float32
        )
        field = (child + jnp.stack([toward_left, toward_right], axis=1)).reshape(
            2 * halves, columns, rank
        )
    return field


def path_rows(matrices, node_ids):
    return jnp.stack(
        [lax.dynamic_index_in_dim(matrices, node, 0, keepdims=False) for node in node_ids], axis=0
    )


def per_device(
    targets,
    points,
    tree_order,
    leaf_basis,
    transfer_local,
    coupling_local,
    transfer_top,
    coupling_top,
):
    start = targets[:, tree_order]
    pts_tree = points[:, tree_order]
    position = lax.axis_index("leaf")
    leaf_count = lax.axis_size("leaf")
    top_depth = leaf_count.bit_length() - 1
    contract_last = (((1,), (1,)), ((), ()))
    node_ids = [
        leaf_count - (leaf_count >> bit_index) + (position >> bit_index + 1)
        for bit_index in range(top_depth)
    ]
    full_transfer, full_coupling = (
        lax.all_gather(transfer_top, "rhs", axis=2, tiled=True),
        lax.all_gather(coupling_top, "rhs", axis=2, tiled=True),
    )
    path_transfer = path_rows(full_transfer, node_ids)
    path_coupling = path_rows(full_coupling, node_ids)

    def totals(values):
        return lax.psum(values, "leaf")

    solution = jnp.zeros_like(start)
    residual = start
    direction = start
    norm_now = totals(jnp.sum(residual * residual, axis=1))
    for repeat in range(ITERS):
        moved = lax.all_to_all(direction, "rhs", split_axis=1, concat_axis=0, tiled=True)
        width = moved.shape[1]
        part_points = lax.dynamic_slice_in_dim(pts_tree, lax.axis_index("rhs") * width, width, 1)
        dense = lax.all_to_all(
            kernel_block(part_points, moved), "rhs", split_axis=0, concat_axis=1, tiled=True
        )
        columns = direction.shape[0]
        leaves_here, leaf_size, rank = leaf_basis.shape
        apply_values = direction.astype(jnp.bfloat16).reshape(columns, leaves_here, leaf_size)
        coeffs = jnp.einsum(
            "cla,lar->lcr", apply_values, leaf_basis, preferred_element_type=jnp.float32
        ).astype(jnp.bfloat16)
        summit, saved = climb(coeffs, transfer_local)
        current = summit[0]
        records = []
        for apply_bit_index in range(top_depth):
            sibling = from_partner(current, "leaf", apply_bit_index)
            on_left = (position >> apply_bit_index) % 2 == 0
            matrix = path_transfer[apply_bit_index]
            link = path_coupling[apply_bit_index]
            records.append((on_left, sibling, matrix, link))
            if apply_bit_index + 1 < top_depth:
                lower = jnp.where(on_left, current, sibling)
                upper = jnp.where(on_left, sibling, current)
                joined = jnp.concatenate([lower, upper], axis=-1)
                current = jnp.dot(joined, matrix, preferred_element_type=jnp.float32).astype(
                    jnp.bfloat16
                )
        top_field = jnp.zeros((columns, rank), jnp.float32)
        for on_left, sibling, matrix, link in reversed(records):
            half_rows = lax.dynamic_slice_in_dim(matrix, jnp.where(on_left, 0, rank), rank, 0)
            child = lax.dot_general(
                top_field.astype(jnp.bfloat16),
                half_rows,
                contract_last,
                preferred_element_type=jnp.float32,
            )
            from_upper = lax.dot_general(
                sibling, link, contract_last, preferred_element_type=jnp.float32
            )
            from_lower = jnp.dot(sibling, link, preferred_element_type=jnp.float32)
            top_field = child + jnp.where(on_left, from_upper, from_lower)
        fields = descend(top_field, saved, transfer_local, coupling_local)
        lowrank = jnp.einsum(
            "lcr,lar->cla",
            fields.astype(jnp.bfloat16),
            leaf_basis,
            preferred_element_type=jnp.float32,
        )
        product_vec = dense + lowrank.reshape(columns, -1)
        step_size = norm_now / totals(jnp.sum(direction * product_vec, axis=1))
        solution = solution + step_size[:, None] * direction
        residual = residual - step_size[:, None] * product_vec
        norm_next = totals(jnp.sum(residual * residual, axis=1))
        direction = residual + (norm_next / norm_now)[:, None] * direction
        norm_now = norm_next
    solution_out = jnp.zeros_like(start).at[:, tree_order].set(solution)
    residual_out = jnp.zeros_like(start).at[:, tree_order].set(residual)
    return (solution_out, residual_out)


def solution(mesh):
    placed = (
        P("rhs", "leaf"),
        P(None, "leaf"),
        P("leaf"),
        P("leaf", None, None),
        P("leaf", None, None),
        P("leaf", None, None),
        P(None, None, "rhs"),
        P(None, None, "rhs"),
    )
    return jax.shard_map(
        per_device,
        mesh=mesh,
        in_specs=placed,
        out_specs=(P("rhs", "leaf"), P("rhs", "leaf")),
        check_vma=False,
    )
```

profile of v0, /device:TPU:1, one launch (start us, length us, event | category | flops | bytes accessed | tf_op | source)
XLA Modules:
  0.0 711.2 jit_solution(6200731693552813525)
XLA Ops:
  8.7 3.4 copy.74
  12.7 29.9 %gather_fusion = f32[8192,4]{1,0:T(8,128)} fusion(f32[4,8192]{0,1:T(8,128)} %copy.74, s32[8192]{0:T(1024)S(1)} %get-tuple-element.26), kind=kCustom, calls=%fused_computation | custom fusion | bytes 294912 | tf_op jit(solution)/shard_map/gather | solution.py:96
  42.7 3.5 copy.75
  49.2 3.2 collective-permute-start
  52.5 3.3 all-to-all-start
  66.8 29.9 %gather_fusion.1 = f32[8192,8]{1,0:T(8,128)} fusion(f32[8,8192]{0,1:T(8,128)} %copy.76, s32[8192]{0:T(1024)S(1)} %get-tuple-element.26), kind=kCustom, calls=%fused_computation.1 | custom fusion | bytes 557056 | tf_op jit(solution)/shard_map/gather | solution.py:97
  98.0 4.7 slice_reduce_fusion.7
  127.3 5.2 fusion.5
  133.3 4.2 all-to-all-start.1
  152.3 2.9 collective-permute-start.4
  157.7 5.3 collective-permute-start.5
  187.6 130.2 %all-reduce = (f32[4]{0:T(128)S(1)}, f32[4]{0:T(128)S(1)}) all-reduce(f32[4]{0:T(128)S(1)} %copy-done.25, f32[4]{0:T(128)S(1)} %multiply_reduce_fusion.1), channel_id=1, replica_groups=mesh['leaf'=64,'rhs'=4] {'leaf'}, use_global_device_ids=true, to_apply=%region_1.2 | all-reduce | flops 8 | bytes 64 | tf_op jit(solution)/shard_map/psum | solution.py:114
  320.6 123.6 %psum.30 = f32[4]{0:T(128)S(1)} all-reduce(f32[4]{0:T(128)S(1)} %multiply_reduce_fusion), channel_id=1, replica_groups=mesh['leaf'=64,'rhs'=4] {'leaf'}, use_global_device_ids=true, to_apply=%region_5.6 | all-reduce | flops 4 | bytes 32 | tf_op jit(solution)/shard_map/psum | solution.py:114
  456.8 4.6 all-to-all-start.2
  467.4 3.0 collective-permute-done.8
  479.1 4.2 collective-permute-start.11
  497.8 5.7 fusion.4
  504.4 4.2 all-to-all-start.3
  509.3 4.2 all-to-all-done.3
  513.7 131.2 %psum.31 = f32[4]{0:T(128)S(1)} all-reduce(f32[4]{0:T(128)S(1)} %fusion.77), channel_id=1, replica_groups=mesh['leaf'=64,'rhs'=4] {'leaf'}, use_global_device_ids=true, to_apply=%region_7.8 | all-reduce | flops 4 | bytes 32 | tf_op jit(solution)/shard_map/psum | solution.py:114
  648.7 23.1 %scatter_custom_fusion = f32[4,8192]{0,1:T(8,128)} fusion(s32[8192]{0:T(1024)} %get-tuple-element.27, f32[8192,4]{1,0:T(8,128)} %copy.110, f32[]{:T(128)} %constant.204.clone.1), kind=kCustom, calls=%fused_computation.7 | custom fusion | bytes 131584 | tf_op jit(solution)/shard_map/scatter | solution.py:177
  671.8 3.5 copy.112
  677.8 23.1 %scatter_custom_fusion.1 = f32[4,8192]{0,1:T(8,128)} fusion(s32[8192]{0:T(1024)} %get-tuple-element.27, f32[8192,4]{1,0:T(8,128)} %copy.111, f32[]{:T(128)} %constant.204.clone.1), kind=kCustom, calls=%fused_computation.5 | custom fusion | bytes 131584 | tf_op jit(solution)/shard_map/scatter | solution.py:178
  700.9 3.5 copy.113
  (221 shorter events, 137.0 us)
Async XLA Ops:
  7.2 40.1 %copy-start = (bf16[32,256,128]{2,1,0:T(8,128)(2,1)S(1)}, bf16[32,256,128]{2,1,0:T(8,128)(2,1)}, u32[]{:S(2)}) copy-start(bf16[32,256,128]{2,1,0:T(8,128)(2,1)} %param.11) | copy-start | bytes 6291460
  7.2 130.4 %all-gather.5.cloned.1.call-start = ((), (), s32[]{:S(2)}) async-start(), calls=%async_computation.5 | async-start | bytes 2580480 | tf_op jit(solution)/shard_map/all_gather | solution.py:108
  7.9 131.1 %all-gather.3.cloned.1.call-start = ((), (), s32[]{:S(2)}) async-start(), calls=%async_computation.4 | async-start | bytes 5160960 | tf_op jit(solution)/shard_map/all_gather | solution.py:107
  49.2 76.2 %collective-permute-start = (bf16[4,128]{1,0:T(4,128)(2,1)}, bf16[4,128]{1,0:T(4,128)(2,1)}, u32[]{:S(2)}, u32[]{:S(2)}) collective-permute-start(bf16[4,128]{1,0:T(4,128)(2,1)} %convolution_convert_fusion.21), channel_id=1, source_target_pairs={{0,4},{4,0},{8,12},{12,8},{16,20},{20,16},{24,28},{28,24},{32,36},... | collective-permute-start | bytes 3080 | tf_op jit(solution)/shard_map/ppermute | solution.py:16
  52.5 74.2 %all-to-all-start = ((f32[4,4,2048]{2,0,1:T(4,128)}), f32[4,4,2048]{2,0,1:T(4,128)S(1)}, u32[]{:S(2)}, u32[]{:S(2)}) async-start(f32[4,4,2048]{2,0,1:T(4,128)} %bitcast.1), calls=%async_computation | async-start | bytes 262144 | tf_op jit(solution)/shard_map/all_to_all | solution.py:121
  132.5 47.9 %copy-start.9 = (f32[16,1,4,128]{3,2,1,0:T(4,128)S(1)}, f32[16,1,4,128]{3,2,1,0:T(4,128)}, u32[]{:S(2)}) copy-start(f32[16,1,4,128]{3,2,1,0:T(4,128)} %convolution_bitcast_fusion.7) | copy-start | bytes 98308
  133.3 52.4 %all-to-all-start.1 = ((f32[4,4,2048]{2,1,0:T(4,128)}), f32[4,4,2048]{2,1,0:T(4,128)S(1)}, u32[]{:S(2)}, u32[]{:S(2)}) async-start(f32[4,4,2048]{2,1,0:T(4,128)} %all_to_all.52), calls=%async_computation.1 | async-start | bytes 262144 | tf_op jit(solution)/shard_map/all_to_all | solution.py:124
  140.0 2.7 collective-permute-start.1
  143.7 3.9 collective-permute-start.2
  148.7 2.6 collective-permute-start.3
  152.3 4.4 collective-permute-start.4
  157.7 6.8 collective-permute-start.5
  317.8 128.1 %copy-start.19 = (f32[4]{0:T(128)}, f32[4]{0:T(128)S(1)}, u32[]{:S(2)}) copy-start(f32[4]{0:T(128)S(1)} %div.9) | copy-start | bytes 52
  453.4 8.0 %collective-permute-start.6 = (bf16[4,128]{1,0:T(4,128)(2,1)}, bf16[4,128]{1,0:T(4,128)(2,1)}, u32[]{:S(2)}, u32[]{:S(2)}) collective-permute-start(bf16[4,128]{1,0:T(4,128)(2,1)} %convolution_convert_fusion.15), channel_id=1, source_target_pairs={{0,4},{4,0},{8,12},{12,8},{16,20},{20,16},{24,28},{28,24},{32,36},... | collective-permute-start | bytes 3080 | tf_op jit(solution)/shard_map/ppermute | solution.py:16
  456.8 40.9 %all-to-all-start.2 = ((f32[4,4,2048]{2,0,1:T(4,128)}), f32[4,4,2048]{2,0,1:T(4,128)S(1)}, u32[]{:S(2)}, u32[]{:S(2)}) async-start(f32[4,4,2048]{2,0,1:T(4,128)} %multiply_add_fusion), calls=%async_computation.2 | async-start | bytes 262144 | tf_op jit(solution)/shard_map/all_to_all | solution.py:121
  463.1 2.4 collective-permute-start.7
  466.5 3.9 collective-permute-start.8
  471.4 2.4 collective-permute-start.9
  474.8 3.3 collective-permute-start.10
  479.1 6.3 collective-permute-start.11
  503.6 141.4 %copy-start.27 = (f32[4]{0:T(128)S(1)}, f32[4]{0:T(128)}, u32[]{:S(2)}) copy-start(f32[4]{0:T(128)} %copy-done.26) | copy-start | bytes 52
  503.6 141.4 %copy-start.21 = (f32[4]{0:T(128)S(1)}, f32[4]{0:T(128)}, u32[]{:S(2)}) copy-start(f32[4]{0:T(128)} %copy-done.19) | copy-start | bytes 52
  503.6 141.4 %copy-start.23 = (f32[4]{0:T(128)S(1)}, f32[4]{0:T(128)}, u32[]{:S(2)}) copy-start(f32[4]{0:T(128)} %copy-done.22) | copy-start | bytes 52
  504.4 9.1 %all-to-all-start.3 = ((f32[4,4,2048]{2,1,0:T(4,128)}), f32[4,4,2048]{2,1,0:T(4,128)S(1)}, u32[]{:S(2)}, u32[]{:S(2)}) async-start(f32[4,4,2048]{2,1,0:T(4,128)} %all_to_all.57), calls=%async_computation.3 | async-start | bytes 262144 | tf_op jit(solution)/shard_map/all_to_all | solution.py:124
  (22 other events, 153.9 us)
Sparse Core Ops, SparseCore 0:
  9.8 36.8 all-gather.4
  48.6 50.2 all-gather.2
where the time goes:
time: 715 us; the launch traced here: 711 us
  blocking collectives  385 us (54%)
  local copies, waits for them, and re-layouts  162 us (23%)
  matrix products  86.1 us (12%)
  starting transfers between devices  36.7 us (5%)
  waiting for transfers between devices  16.7 us (2%)
  between operations  14.4 us (2%)
  other arithmetic  10.9 us (2%)
    psum x3, blocking collectives, totals(): return lax.psum(values, 'leaf')  385 us
    gather x2, local copies, waits for them, and re-layouts, per_device(): start = targets[:, tree_order]  33.4 us
    gather x1, local copies, waits for them, and re-layouts, per_device(): pts_tree = points[:, tree_order]  29.9 us
    scatter x1, local copies, waits for them, and re-layouts, per_device(): solution_out = jnp.zeros_like(start).at[:, tree_order].set(solution)  23.1 us
    scatter x1, local copies, waits for them, and re-layouts, per_device(): residual_out = jnp.zeros_like(start).at[:, tree_order].set(residual)  23.1 us
    ppermute x12, starting transfers between devices, from_partner(): lax.ppermute(shard, axis, [(i, i ^ 1 << stride) for i in range(lax.axis_s...  20.2 us
    unnamed x62, local copies, waits for them, and re-layouts  15.7 us
    dot_general x11, matrix products, per_device(): lax.dot_general(top_field.astype(jnp.bfloat16), half_rows, contract_last,...  15.5 us
  transfers between devices with their start and end apart: 18, of which 8 were waited for; matrix products, arithmetic and copies ran while one was open for 25% of the time, Pallas kernels for 0%

commit v1 on v0

v1 whole, which is shorter than its diff:
```python
import functools

import jax
import jax.numpy as jnp
from jax import lax
from jax.experimental import pallas as pl
from jax.experimental.pallas import tpu as pltpu
from jax.sharding import PartitionSpec as P

LEAF = 256
RANK = 128
DIMS = 8
ROWS = 8
kernel_rate = 0.0625
ridge_term = 1.0

f32 = jnp.float32
bf16 = jnp.bfloat16
MESH = pl.DeviceIdType.MESH
ROUNDS = 8


def rounded(values):
    return values.astype(bf16).astype(f32)


def batched(left, right):
    return lax.dot_general(left, right, (((2,), (1,)), ((0,), (0,))), preferred_element_type=f32)


def batched_t(left, right):
    return lax.dot_general(left, right, (((2,), (2,)), ((0,), (0,))), preferred_element_type=f32)


def up_level(coeffs, matrices, multiply=batched):
    half = coeffs.shape[0] // 2
    paired = coeffs.reshape(half, 2, ROWS, RANK)
    joined = jnp.concatenate([paired[:, 0], paired[:, 1]], axis=-1).astype(bf16)
    return rounded(multiply(joined, matrices)), paired


def whole_kernel(
    sizes,
    tgt_ref,
    pts_ref,
    idx_ref,
    basis_hbm,
    transfer_hbm,
    coupling_hbm,
    ttop_hbm,
    ctop_hbm,
    sol_ref,
    res_ref,
    basis,
    transfer,
    coupling,
    top_t,
    top_c,
    lhs_t32,
    lhs_t,
    lhs_p,
    onehot,
    k_high,
    k_low,
    vec,
    dense,
    image,
    first,
    acc,
    links,
    slots,
    load_sem,
    x_send,
    x_recv,
    t_send,
    t_recv,
):
    spread, group, planes, leaves = sizes
    leaf = lax.axis_index("leaf")
    mine = lax.axis_index("rhs")
    inner = lax.rem(leaf, group)
    plane = leaf // group
    base = plane * group

    barrier = pltpu.get_barrier_semaphore()

    def greet_inner(j, carry):
        other = base + lax.rem(inner + j, group)
        pl.semaphore_signal(barrier, inc=1, device_id=(other, mine), device_id_type=MESH)
        return carry

    def greet_plane(j, carry):
        other = inner + group * lax.rem(plane + j, planes)
        pl.semaphore_signal(barrier, inc=1, device_id=(other, mine), device_id_type=MESH)
        return carry

    def greet_x(j, carry):
        other = lax.rem(mine + j, spread)
        pl.semaphore_signal(barrier, inc=1, device_id=(leaf, other), device_id_type=MESH)
        return carry

    lax.fori_loop(1, group, greet_inner, 0)
    lax.fori_loop(1, planes, greet_plane, 0)
    lax.fori_loop(1, spread, greet_x, 0)

    width = RANK // spread
    mine_rows = pl.ds(pl.multiple_of(mine * width, width), width)
    tops = []
    low_levels = group.bit_length() - 1
    high_levels = planes.bit_length() - 1
    count = group * planes
    place = 0
    first_node = 0
    for level in range(low_levels):
        here = group >> level + 1
        tops.append((first_node + plane * here, place, here))
        place += here
        first_node += count >> level + 1
    tops.append((first_node, place, planes - 1))
    place += planes - 1
    nodes = place
    top_loads = []
    for i, (source, target, number) in enumerate(tops):
        for hbm, top, k in ((ttop_hbm, top_t, 0), (ctop_hbm, top_c, 1)):
            copy = pltpu.make_async_copy(
                hbm.at[pl.ds(source, number)],
                top.at[pl.ds(target, number), mine_rows],
                load_sem.at[3 + 2 * i + k],
            )
            copy.start()
            top_loads.append(copy)
    load_basis = pltpu.make_async_copy(basis_hbm, basis, load_sem.at[0])
    load_transfer = pltpu.make_async_copy(transfer_hbm, transfer, load_sem.at[1])
    load_coupling = pltpu.make_async_copy(coupling_hbm, coupling, load_sem.at[2])
    load_basis.start()
    load_transfer.start()
    load_coupling.start()
    pl.semaphore_wait(barrier, group - 1 + planes - 1 + spread - 1)

    def x_copies(owner, j, other):
        own_rows = pl.ds(pl.multiple_of(owner * width, width), width)
        return [
            pltpu.make_async_remote_copy(
                src_ref=top.at[:, own_rows],
                dst_ref=top.at[:, own_rows],
                send_sem=x_send.at[k, j - 1],
                recv_sem=x_recv.at[k, owner],
                device_id=(leaf, other),
                device_id_type=MESH,
            )
            for k, top in enumerate((top_t, top_c))
        ]

    for copy in top_loads:
        copy.wait()

    def x_start(j, carry):
        for copy in x_copies(mine, j, lax.rem(mine + j, spread)):
            copy.start()
        return carry

    lax.fori_loop(1, spread, x_start, 0)

    def tile_copy(turn, slot, j, other):
        return pltpu.make_async_remote_copy(
            src_ref=slots.at[turn, slot],
            dst_ref=slots.at[turn, slot],
            send_sem=t_send.at[turn, j - 1],
            recv_sem=t_recv.at[turn, slot],
            device_id=(other, mine),
            device_id_type=MESH,
        )

    def partner(turn, j):
        if turn % 2 == 0:
            slot = lax.rem(inner + j, group)
            return slot, base + slot
        slot = lax.rem(plane + j, planes)
        return slot, inner + group * slot

    def exchange_start(turn, tile):
        me, number = (inner, group) if turn % 2 == 0 else (plane, planes)
        slots[turn, me] = tile

        def step(j, carry):
            tile_copy(turn, me, j, partner(turn, j)[1]).start()
            return carry

        lax.fori_loop(1, number, step, 0)

    def exchange_wait(turn):
        number = group if turn % 2 == 0 else planes

        def step(j, carry):
            slot, other = partner(turn, j)
            tile_copy(turn, slot, j, other).wait_recv()
            return carry

        lax.fori_loop(1, number, step, 0)
        return slots[turn, :number]

    for h in range(leaves):
        piece = tgt_ref[:, h * LEAF : (h + 1) * LEAF]
        high = rounded(piece)
        lhs_t32[h * 8 : h * 8 + 4, :] = high
        lhs_t32[h * 8 + 4 : h * 8 + 8, :] = piece - high
        piece = pts_ref[:, h * LEAF : (h + 1) * LEAF]
        high = rounded(piece)
        lhs_p[h * 16 : (h + 1) * 16, :] = jnp.concatenate([high, piece - high], axis=0).astype(bf16)
    lhs_t[...] = lhs_t32[...].astype(bf16)

    def index_row(c):
        return jnp.concatenate(
            [idx_ref[pl.ds(2 * c, 1), :], idx_ref[pl.ds(2 * c + 1, 1), :]], axis=1
        )

    def gather_leaf(c, carry):
        order = index_row(c)
        low = lax.bitwise_and(order, LEAF - 1)
        high = lax.shift_right_logical(order, 8)
        hot = lax.broadcasted_iota(jnp.int32, (LEAF, LEAF), 0) == low
        hot = jnp.where(hot, 1.0, 0.0).astype(bf16)
        onehot[c] = hot
        rows_t = jnp.dot(lhs_t[...], hot, preferred_element_type=f32).reshape(leaves, 8, LEAF)
        rows_p = jnp.dot(lhs_p[...], hot, preferred_element_type=f32).reshape(leaves, 16, LEAF)
        here_t = lax.broadcasted_iota(jnp.int32, (leaves, 8, LEAF), 0) == high[None]
        here_p = lax.broadcasted_iota(jnp.int32, (leaves, 16, LEAF), 0) == high[None]
        both = jnp.sum(jnp.where(here_t, rows_t, 0.0), axis=0)
        spots = jnp.sum(jnp.where(here_p, rows_p, 0.0), axis=0)
        vec[c] = both + pltpu.roll(both, 4, 0)
        spot_high, spot_low = spots[:8], spots[8:]
        whole = spot_high + spot_low
        norm = jnp.sum(whole * whole, axis=0, keepdims=True) * -kernel_rate
        norm_a = rounded(norm)
        norm_b = rounded(norm - norm_a)
        norm_c = norm - norm_a - norm_b
        row = lax.broadcasted_iota(jnp.int32, (8, LEAF), 0)
        norms = jnp.where(row == 0, norm_a, jnp.where(row == 1, norm_b, norm_c))
        ones = jnp.ones((8, LEAF), f32)
        zeros = jnp.zeros((8, LEAF), f32)
        tail_left = jnp.where(row < 3, norms, jnp.where(row < 6, ones, zeros))
        norms_up = jnp.where(row == 3, norm_a, jnp.where(row == 4, norm_b, norm_c))
        tail_right = jnp.where(row < 3, ones, jnp.where(row < 6, norms_up, zeros))
        left = jnp.concatenate(
            [spot_high, spot_high, spot_low, spot_low, tail_left, zeros], axis=0
        ).astype(bf16)
        right_high = spot_high * (2 * kernel_rate)
        right_low = spot_low * (2 * kernel_rate)
        right = jnp.concatenate(
            [right_high, right_low, right_high, right_low, tail_right, zeros], axis=0
        ).astype(bf16)
        power = lax.dot_general(left, right, (((0,), (0,)), ((), ())), preferred_element_type=f32)
        values = jnp.exp(power)
        values_high = values.astype(bf16)
        k_high[c] = values_high
        k_low[c] = (values - values_high.astype(f32)).astype(bf16)
        return carry

    lax.fori_loop(0, leaves, gather_leaf, 0)

    def x_wait(j, carry):
        other = lax.rem(mine + j, spread)
        for copy in x_copies(other, j, other):
            copy.wait_recv()
        return carry

    lax.fori_loop(1, spread, x_wait, 0)

    row8 = lax.broadcasted_iota(jnp.int32, (ROWS, RANK), 0)
    upper = row8 < 4

    def swap(tile):
        return pltpu.roll(tile, 4, 0)

    def lane_partial(product):
        total = jnp.sum(product, axis=0)
        return total[:, :RANK] + total[:, RANK:]

    def full(tile):
        return jnp.broadcast_to(jnp.sum(tile, axis=1, keepdims=True), (ROWS, RANK))

    def wide_of(tile):
        return jnp.concatenate([tile, tile], axis=1)[None]

    def apply_matrix(turn):
        value = vec[...]
        square = lane_partial(value * value)
        coeffs = rounded(batched(value.astype(bf16), basis[...]))
        saved = []
        offset = 0
        number = leaves
        while number > 1:
            half = number // 2
            coeffs, paired = up_level(coeffs, transfer[offset : offset + half])
            saved.append((paired, offset, half))
            offset += half
            number = half
        exchange_start(turn, jnp.where(upper, coeffs[0], square))

        high = rounded(value)
        sub_row = lax.broadcasted_iota(jnp.int32, value.shape, 1)
        stacked = jnp.where(sub_row < 4, high, value - high).astype(bf16)
        product = batched(stacked, k_high[...]) + batched(stacked, k_low[...])
        dense[...] = product + pltpu.roll(product, 4, 1) + ridge_term * value

        tiles = exchange_wait(turn)
        group_square = jnp.sum(tiles, axis=0)
        levels = [tiles]
        place = 0
        while levels[-1].shape[0] > 1:
            half = levels[-1].shape[0] // 2
            levels.append(up_level(levels[-1], top_t[place : place + half], batched_t)[0])
            place += half
        exchange_start(turn + 1, jnp.where(upper, levels.pop()[0], group_square))

        for paired, offset, half in saved:
            matrices = coupling[offset : offset + half]
            links[0, offset : offset + half] = batched_t(paired[:, 1].astype(bf16), matrices)
            links[1, offset : offset + half] = batched(paired[:, 0].astype(bf16), matrices)

        tiles = exchange_wait(turn + 1)
        total_square = jnp.sum(tiles, axis=0)
        levels.append(tiles)
        while levels[-1].shape[0] > 2:
            half = levels[-1].shape[0] // 2
            levels.append(up_level(levels[-1], top_t[place : place + half], batched_t)[0])
            place += half

        field = None
        place = nodes
        for level in reversed(range(low_levels + high_levels)):
            if level >= low_levels:
                number = planes >> level - low_levels + 1
            else:
                number = group >> level + 1
            place -= number
            spot = plane if level >= low_levels else inner
            depth = level - low_levels if level >= low_levels else level
            node = lax.shift_right_logical(spot, depth + 1)
            side = lax.bitwise_and(lax.shift_right_logical(spot, depth), 1)
            pairs = levels[level]
            sibling = jnp.zeros((ROWS, RANK), f32)
            for k in range(pairs.shape[0]):
                chosen = lax.shift_right_logical(spot, depth) + 1 - 2 * side == k
                sibling = jnp.where(chosen, pairs[k], sibling)
            sibling = sibling.astype(bf16)
            link = top_c[place + node]
            to_left = jnp.dot(sibling, link, preferred_element_type=f32)
            to_right = lax.dot_general(
                sibling, link, (((1,), (1,)), ((), ())), preferred_element_type=f32
            )
            own = jnp.where(side == 0, to_left, to_right)
            if field is not None:
                half_lanes = pl.multiple_of(side * RANK, RANK)
                half = top_t[place + node, :, pl.ds(half_lanes, RANK)]
                own = own + jnp.dot(field.astype(bf16), half, preferred_element_type=f32)
            field = own
        field = jnp.where(upper, field, swap(field))[None]

        for _, offset, half in reversed(saved):
            child = batched_t(field.astype(bf16), transfer[offset : offset + half])
            left = child[:, :, :RANK] + links[0, offset : offset + half]
            right = child[:, :, RANK:] + links[1, offset : offset + half]
            field = jnp.stack([left, right], axis=1).reshape(2 * half, ROWS, RANK)
        image[...] = dense[...] + batched_t(field.astype(bf16), basis[...])
        total_square = full(total_square)
        return jnp.where(upper, swap(total_square), total_square)

    def reduce_all(turn, partial):
        exchange_start(turn, partial)
        total = jnp.sum(exchange_wait(turn), axis=0)
        exchange_start(turn + 1, total)
        return full(jnp.sum(exchange_wait(turn + 1), axis=0))

    load_basis.wait()
    load_transfer.wait()
    load_coupling.wait()

    rr_first = apply_matrix(0)
    start = vec[...]
    step_size = rr_first / reduce_all(2, lane_partial(start * image[...]))
    first[0] = start
    first[1] = image[...]
    vec[...] = start - wide_of(step_size) * image[...]

    rr_second = apply_matrix(4)
    ratio = wide_of(rr_second / rr_first)
    residual = vec[...]
    direction = residual + ratio * first[0]
    image[...] = image[...] + ratio * first[1]
    last_size = rr_second / reduce_all(6, lane_partial(direction * image[...]))
    solution = wide_of(step_size) * first[0] + wide_of(last_size) * direction
    residual = residual - wide_of(last_size) * image[...]
    sub_row = lax.broadcasted_iota(jnp.int32, residual.shape, 1)
    vec[...] = jnp.where(sub_row < 4, solution, residual)

    acc[...] = jnp.zeros_like(acc)

    def scatter_leaf(c, carry):
        order = index_row(c)
        high = lax.shift_right_logical(order, 8)
        here = lax.broadcasted_iota(jnp.int32, (leaves, 8, LEAF), 0) == high[None]
        value = vec[c]
        value_high = rounded(value)
        value_low = value - value_high
        part_high = jnp.where(here, value_high[None], 0.0).reshape(leaves * 8, LEAF)
        part_low = jnp.where(here, value_low[None], 0.0).reshape(leaves * 8, LEAF)
        rows = jnp.concatenate([part_high, part_low], axis=0).astype(bf16)
        acc[...] += lax.dot_general(
            rows, onehot[c], (((1,), (1,)), ((), ())), preferred_element_type=f32
        )
        return carry

    lax.fori_loop(0, leaves, scatter_leaf, 0)
    for h in range(leaves):
        tile = acc[h * 8 : h * 8 + 8, :] + acc[leaves * 8 + h * 8 : leaves * 8 + h * 8 + 8, :]
        sol_ref[:, h * LEAF : (h + 1) * LEAF] = tile[:4]
        res_ref[:, h * LEAF : (h + 1) * LEAF] = tile[4:]

    def x_done(j, carry):
        for copy in x_copies(mine, j, lax.rem(mine + j, spread)):
            copy.wait_send()
        return carry

    lax.fori_loop(1, spread, x_done, 0)
    for turn in range(ROUNDS):
        me, number = (inner, group) if turn % 2 == 0 else (plane, planes)

        def sent(j, carry):
            tile_copy(turn, me, j, partner(turn, j)[1]).wait_send()
            return carry

        lax.fori_loop(1, number, sent, 0)


def per_device(
    targets,
    points,
    tree_order,
    leaf_basis,
    transfer_local,
    coupling_local,
    transfer_top,
    coupling_top,
):
    spread = lax.axis_size("rhs")
    count = lax.axis_size("leaf")
    bits = count.bit_length() - 1
    group = 1 << (bits + 1) // 2
    planes = count // group
    leaves = leaf_basis.shape[0]
    columns, here = targets.shape
    nodes = group - 1 + planes - 1
    loads = 3 + 2 * (group.bit_length())
    most = max(group, planes)
    vmem = pl.BlockSpec(memory_space=pltpu.VMEM)
    any_space = pl.BlockSpec(memory_space=pl.ANY)
    out = jax.ShapeDtypeStruct((columns, here), f32)
    return pl.pallas_call(
        functools.partial(whole_kernel, (spread, group, planes, leaves)),
        out_shape=(out, out),
        in_specs=[vmem, vmem, vmem] + [any_space] * 5,
        out_specs=(vmem, vmem),
        scratch_shapes=[
            pltpu.VMEM(leaf_basis.shape, bf16),
            pltpu.VMEM(transfer_local.shape, bf16),
            pltpu.VMEM(coupling_local.shape, bf16),
            pltpu.VMEM((nodes, RANK, 2 * RANK), bf16),
            pltpu.VMEM((nodes, RANK, RANK), bf16),
            pltpu.VMEM((leaves * 8, LEAF), f32),
            pltpu.VMEM((leaves * 8, LEAF), bf16),
            pltpu.VMEM((leaves * 16, LEAF), bf16),
            pltpu.VMEM((leaves, LEAF, LEAF), bf16),
            pltpu.VMEM((leaves, LEAF, LEAF), bf16),
            pltpu.VMEM((leaves, LEAF, LEAF), bf16),
            pltpu.VMEM((leaves, ROWS, LEAF), f32),
            pltpu.VMEM((leaves, ROWS, LEAF), f32),
            pltpu.VMEM((leaves, ROWS, LEAF), f32),
            pltpu.VMEM((2, leaves, ROWS, LEAF), f32),
            pltpu.VMEM((2 * leaves * 8, LEAF), f32),
            pltpu.VMEM((2, leaves - 1, ROWS, RANK), f32),
            pltpu.VMEM((ROUNDS, most, ROWS, RANK), f32),
            pltpu.SemaphoreType.DMA((loads,)),
            pltpu.SemaphoreType.DMA((2, spread - 1)),
            pltpu.SemaphoreType.DMA((2, spread)),
            pltpu.SemaphoreType.DMA((ROUNDS, most - 1)),
            pltpu.SemaphoreType.DMA((ROUNDS, most)),
        ],
        compiler_params=pltpu.CompilerParams(
            collective_id=0, has_side_effects=True, vmem_limit_bytes=56 * 1024 * 1024
        ),
        name="ridge",
    )(
        targets,
        points,
        tree_order.reshape(-1, RANK),
        leaf_basis,
        transfer_local,
        coupling_local,
        transfer_top.transpose(0, 2, 1),
        coupling_top.transpose(0, 2, 1),
    )


def solution(mesh):
    placed = (
        P("rhs", "leaf"),
        P(None, "leaf"),
        P("leaf"),
        P("leaf", None, None),
        P("leaf", None, None),
        P("leaf", None, None),
        P(None, None, "rhs"),
        P(None, None, "rhs"),
    )
    return jax.shard_map(
        per_device,
        mesh=mesh,
        in_specs=placed,
        out_specs=(P("rhs", "leaf"), P("rhs", "leaf")),
        check_vma=False,
    )
```

time: 715 us -> 83.1 us (0.12)
  blocking collectives: 385 us -> 0 us
  local copies, waits for them, and re-layouts: 162 us -> 3.14 us
  matrix products: 86.1 us -> 0 us
  Pallas kernels: 0 us -> 79.1 us
  starting transfers between devices: 36.7 us -> 0 us
  waiting for transfers between devices: 16.7 us -> 0 us
  between operations: 14.4 us -> 0.64 us
  other arithmetic: 10.9 us -> 0 us
    psum x3 -> x0, blocking collectives: 385 us -> none  [totals(): return lax.psum(values, 'leaf')]
    dot_general x79 -> x0, matrix products: 86.1 us -> none  [the longest x11 15.5 us: per_device(): lax.dot_general(top_field.astype(jnp.bfloat16), half_rows, contract_last,...]
    pallas_call x0 -> x1, Pallas kernels: none -> 79.1 us  [per_device(): pl.pallas_call(functools.partial(whole_kernel, (spread, group, planes, le...]
    gather x3 -> x0, local copies, waits for them, and re-layouts: 63.3 us -> none  [the longest x2 33.4 us: per_device(): start = targets[:, tree_order]]
    scatter x2 -> x0, local copies, waits for them, and re-layouts: 46.1 us -> none  [the longest x1 23.1 us: per_device(): solution_out = jnp.zeros_like(start).at[:, tree_order].set(solution)]
    ppermute x12 -> x0, starting transfers between devices: 20.2 us -> none  [from_partner(): lax.ppermute(shard, axis, [(i, i ^ 1 << stride) for i in range(lax.axis_s...]
    all_to_all x4 -> x0, starting transfers between devices: 16.5 us -> none  [the longest x2 8.47 us: per_device(): lax.all_to_all(kernel_block(part_points, moved), 'rhs', split_axis=0, con...]
    slice x6 -> x0, local copies, waits for them, and re-layouts: 13.1 us -> none  [the longest x5 8.34 us: descend(): matrices = transfer[offset:offset + halves].reshape(halves, 2, rank, rank)]
  transfers between devices with their start and end apart: 18 -> 0, of which waited for: 8 -> 0; matrix products, arithmetic and copies ran while one was open for 25% -> 0% of each run, Pallas kernels for 0% -> 0%
where the time goes in v1:
time: 83.1 us; the launch traced here: 82.9 us
  Pallas kernels  79.1 us (95%)
  local copies, waits for them, and re-layouts  3.14 us (4%)
    pallas_call x1, Pallas kernels, per_device(): pl.pallas_call(functools.partial(whole_kernel, (spread, group, planes, le...  79.1 us
    unnamed x2, local copies, waits for them, and re-layouts  3.14 us

profile of v1, /device:TPU:1, one launch (start us, length us, event | category | flops | bytes accessed | tf_op | source)
XLA Modules:
  0.0 82.9 jit_solution(8781980996603248032)
XLA Ops:
  0.6 79.1 %ridge.1 = (f32[4,8192]{1,0:T(4,128)}, f32[4,8192]{1,0:T(4,128)}) custom-call(f32[4,8192]{1,0:T(4,128)} %tgt_ref.1, f32[8,8192]{1,0:T(8,128)} %pts_ref.1, s32[64,128]{1,0:T(8,128)} %bitcast.5, bf16[32,256,128]{2,1,0:T(8,128)(2,1)} %basis_hbm.1, bf16[31,256,128]{2,1,0:T(8,128)(2,1)} %transfer_hbm.1, bf16[31,128,128]{2,1,0:T(8,128)(2,1)} %coupling_hbm.1, ...), custom_call_target="tpu_custom_call" | custom-call | tf_op jit(solution)/shard_map/ridge/pallas_call | solution.py:459
  79.8 1.6 %copy.12 = f32[4,8192]{1,0:T(4,128)} copy(f32[4,8192]{1,0:T(4,128)} %get-tuple-element.4) | data formatting | bytes 262144
  81.4 1.6 %copy.13 = f32[4,8192]{1,0:T(4,128)} copy(f32[4,8192]{1,0:T(4,128)} %get-tuple-element.5) | data formatting | bytes 262144

commit v2 on v1

--- a/solution.py
+++ b/solution.py
@@ -137,29 +137,38 @@
     load_coupling.start()
     pl.semaphore_wait(barrier, group - 1 + planes - 1 + spread - 1)
 
-    def x_copies(owner, j, other):
+    low_nodes = group - 1
+    parts = (pl.ds(0, low_nodes), pl.ds(low_nodes, nodes - low_nodes))
+
+    def x_copies(part, owner, j, other):
         own_rows = pl.ds(pl.multiple_of(owner * width, width), width)
         return [
             pltpu.make_async_remote_copy(
-                src_ref=top.at[:, own_rows],
-                dst_ref=top.at[:, own_rows],
-                send_sem=x_send.at[k, j - 1],
-                recv_sem=x_recv.at[k, owner],
+                src_ref=top.at[parts[part], own_rows],
+                dst_ref=top.at[parts[part], own_rows],
+                send_sem=x_send.at[2 * part + k, j - 1],
+                recv_sem=x_recv.at[2 * part + k, owner],
                 device_id=(leaf, other),
                 device_id_type=MESH,
             )
             for k, top in enumerate((top_t, top_c))
         ]
 
-    for copy in top_loads:
-        copy.wait()
-
-    def x_start(j, carry):
-        for copy in x_copies(mine, j, lax.rem(mine + j, spread)):
-            copy.start()
-        return carry
-
-    lax.fori_loop(1, spread, x_start, 0)
+    def far_first(number):
+        return sorted(range(1, number), key=lambda j: (-min(j, number - j), j))
+
+    for part in range(2):
+        for copy in top_loads[: 2 * low_levels] if part == 0 else top_loads[2 * low_levels :]:
+            copy.wait()
+        for j in far_first(spread):
+            for copy in x_copies(part, mine, j, lax.rem(mine + j, spread)):
+                copy.start()
+
+    def x_wait(part):
+        for j in far_first(spread):
+            other = lax.rem(mine + j, spread)
+            for copy in x_copies(part, other, j, other):
+                copy.wait_recv()
 
     def tile_copy(turn, slot, j, other):
         return pltpu.make_async_remote_copy(
@@ -181,22 +190,14 @@
     def exchange_start(turn, tile):
         me, number = (inner, group) if turn % 2 == 0 else (plane, planes)
         slots[turn, me] = tile
-
-        def step(j, carry):
+        for j in far_first(number):
             tile_copy(turn, me, j, partner(turn, j)[1]).start()
-            return carry
-
-        lax.fori_loop(1, number, step, 0)
 
     def exchange_wait(turn):
         number = group if turn % 2 == 0 else planes
-
-        def step(j, carry):
+        for j in reversed(far_first(number)):
             slot, other = partner(turn, j)
             tile_copy(turn, slot, j, other).wait_recv()
-            return carry
-
-        lax.fori_loop(1, number, step, 0)
         return slots[turn, :number]
 
     for h in range(leaves):
@@ -256,15 +257,7 @@
         k_low[c] = (values - values_high.astype(f32)).astype(bf16)
         return carry
 
-    lax.fori_loop(0, leaves, gather_leaf, 0)
-
-    def x_wait(j, carry):
-        other = lax.rem(mine + j, spread)
-        for copy in x_copies(other, j, other):
-            copy.wait_recv()
-        return carry
-
-    lax.fori_loop(1, spread, x_wait, 0)
+    lax.fori_loop(0, leaves, gather_leaf, 0, unroll=4)
 
     row8 = lax.broadcasted_iota(jnp.int32, (ROWS, RANK), 0)
     upper = row8 < 4
@@ -282,7 +275,32 @@
     def wide_of(tile):
         return jnp.concatenate([tile, tile], axis=1)[None]
 
-    def apply_matrix(turn):
+    def both_halves(tile):
+        return jnp.where(upper, tile, swap(tile))
+
+    def level_links(level, pairs, place):
+        spot, depth = (plane, level - low_levels) if level >= low_levels else (inner, level)
+        node = lax.shift_right_logical(spot, depth + 1)
+        side = lax.bitwise_and(lax.shift_right_logical(spot, depth), 1)
+        sibling = jnp.zeros((ROWS, RANK), f32)
+        for k in range(pairs.shape[0]):
+            chosen = lax.shift_right_logical(spot, depth) + 1 - 2 * side == k
+            sibling = jnp.where(chosen, pairs[k], sibling)
+        sibling = sibling.astype(bf16)
+        link = top_c[place + node]
+        to_left = jnp.dot(sibling, link, preferred_element_type=f32)
+        to_right = lax.dot_general(
+            sibling, link, (((1,), (1,)), ((), ())), preferred_element_type=f32
+        )
+        return jnp.where(side == 0, to_left, to_right), side, place + node
+
+    def level_product(pairs, place):
+        half = pairs.shape[0] // 2
+        paired = pairs.reshape(half, 2, ROWS, RANK)
+        toward = batched(paired[:, 1].astype(bf16), top_c[place : place + half])
+        return jnp.sum(paired[:, 0] * toward, axis=0)
+
+    def apply_matrix(turn, extra):
         value = vec[...]
         square = lane_partial(value * value)
         coeffs = rounded(batched(value.astype(bf16), basis[...]))
@@ -301,61 +319,60 @@
         sub_row = lax.broadcasted_iota(jnp.int32, value.shape, 1)
         stacked = jnp.where(sub_row < 4, high, value - high).astype(bf16)
         product = batched(stacked, k_high[...]) + batched(stacked, k_low[...])
-        dense[...] = product + pltpu.roll(product, 4, 1) + ridge_term * value
-
+        product = product + pltpu.roll(product, 4, 1) + ridge_term * value
+        dense[...] = product
+        inside = jnp.zeros((ROWS, RANK), f32)
+        for paired, offset, half in saved:
+            matrices = coupling[offset : offset + half]
+            toward = batched_t(paired[:, 1].astype(bf16), matrices)
+            links[0, offset : offset + half] = toward
+            links[1, offset : offset + half] = batched(paired[:, 0].astype(bf16), matrices)
+            inside = inside + jnp.sum(paired[:, 0] * toward, axis=0)
+        inside = 2.0 * inside + lane_partial(value * product)
+        exchange_start(turn + 2, jnp.where(upper, inside, extra))
+
+        if turn == 0:
+            x_wait(0)
         tiles = exchange_wait(turn)
         group_square = jnp.sum(tiles, axis=0)
         levels = [tiles]
+        starts = [0]
         place = 0
-        while levels[-1].shape[0] > 1:
+        for level in range(low_levels):
             half = levels[-1].shape[0] // 2
             levels.append(up_level(levels[-1], top_t[place : place + half], batched_t)[0])
             place += half
+            starts.append(place)
         exchange_start(turn + 1, jnp.where(upper, levels.pop()[0], group_square))
 
-        for paired, offset, half in saved:
-            matrices = coupling[offset : offset + half]
-            links[0, offset : offset + half] = batched_t(paired[:, 1].astype(bf16), matrices)
-            links[1, offset : offset + half] = batched(paired[:, 0].astype(bf16), matrices)
-
+        owns = [level_links(level, levels[level], starts[level]) for level in range(low_levels)]
+        inside = jnp.zeros((ROWS, RANK), f32)
+        for level in range(low_levels):
+            inside = inside + level_product(levels[level], starts[level])
+        group_sums = jnp.sum(exchange_wait(turn + 2), axis=0)
+        exchange_start(turn + 3, group_sums + jnp.where(upper, 2.0 * inside, 0.0))
+
+        if turn == 0:
+            x_wait(1)
         tiles = exchange_wait(turn + 1)
         total_square = jnp.sum(tiles, axis=0)
         levels.append(tiles)
-        while levels[-1].shape[0] > 2:
+        for level in range(high_levels - 1):
             half = levels[-1].shape[0] // 2
             levels.append(up_level(levels[-1], top_t[place : place + half], batched_t)[0])
             place += half
+            starts.append(place)
+        for level in range(low_levels, low_levels + high_levels):
+            owns.append(level_links(level, levels[level], starts[level]))
 
         field = None
-        place = nodes
-        for level in reversed(range(low_levels + high_levels)):
-            if level >= low_levels:
-                number = planes >> level - low_levels + 1
-            else:
-                number = group >> level + 1
-            place -= number
-            spot = plane if level >= low_levels else inner
-            depth = level - low_levels if level >= low_levels else level
-            node = lax.shift_right_logical(spot, depth + 1)
-            side = lax.bitwise_and(lax.shift_right_logical(spot, depth), 1)
-            pairs = levels[level]
-            sibling = jnp.zeros((ROWS, RANK), f32)
-            for k in range(pairs.shape[0]):
-                chosen = lax.shift_right_logical(spot, depth) + 1 - 2 * side == k
-                sibling = jnp.where(chosen, pairs[k], sibling)
-            sibling = sibling.astype(bf16)
-            link = top_c[place + node]
-            to_left = jnp.dot(sibling, link, preferred_element_type=f32)
-            to_right = lax.dot_general(
-                sibling, link, (((1,), (1,)), ((), ())), preferred_element_type=f32
-            )
-            own = jnp.where(side == 0, to_left, to_right)
+        for own, side, node in reversed(owns):
             if field is not None:
                 half_lanes = pl.multiple_of(side * RANK, RANK)
-                half = top_t[place + node, :, pl.ds(half_lanes, RANK)]
+                half = top_t[node, :, pl.ds(half_lanes, RANK)]
                 own = own + jnp.dot(field.astype(bf16), half, preferred_element_type=f32)
             field = own
-        field = jnp.where(upper, field, swap(field))[None]
+        field = both_halves(field)[None]
 
         for _, offset, half in reversed(saved):
             child = batched_t(field.astype(bf16), transfer[offset : offset + half])
@@ -363,34 +380,40 @@
             right = child[:, :, RANK:] + links[1, offset : offset + half]
             field = jnp.stack([left, right], axis=1).reshape(2 * half, ROWS, RANK)
         image[...] = dense[...] + batched_t(field.astype(bf16), basis[...])
+
+        inside = jnp.zeros((ROWS, RANK), f32)
+        for level in range(low_levels, low_levels + high_levels):
+            inside = inside + level_product(levels[level], starts[level])
+        sums = jnp.sum(exchange_wait(turn + 3), axis=0)
+        sums = full(sums + jnp.where(upper, 2.0 * inside, 0.0))
         total_square = full(total_square)
-        return jnp.where(upper, swap(total_square), total_square)
-
-    def reduce_all(turn, partial):
-        exchange_start(turn, partial)
-        total = jnp.sum(exchange_wait(turn), axis=0)
-        exchange_start(turn + 1, total)
-        return full(jnp.sum(exchange_wait(turn + 1), axis=0))
+        return (
+            jnp.where(upper, swap(total_square), total_square),
+            both_halves(sums),
+            jnp.where(upper, swap(sums), sums),
+        )
 
     load_basis.wait()
     load_transfer.wait()
     load_coupling.wait()
 
-    rr_first = apply_matrix(0)
+    rr_first, curve_first, _ = apply_matrix(0, jnp.zeros((ROWS, RANK), f32))
+    step_size = rr_first / curve_first
     start = vec[...]
-    step_size = rr_first / reduce_all(2, lane_partial(start * image[...]))
+    product = image[...]
     first[0] = start
-    first[1] = image[...]
-    vec[...] = start - wide_of(step_size) * image[...]
-
-    rr_second = apply_matrix(4)
-    ratio = wide_of(rr_second / rr_first)
+    first[1] = product
+    residual = start - wide_of(step_size) * product
+    vec[...] = residual
+
+    rr_second, curve, cross = apply_matrix(4, lane_partial(residual * product))
+    ratio = rr_second / rr_first
+    last_size = rr_second / (curve + 2.0 * ratio * cross + ratio * ratio * curve_first)
     residual = vec[...]
-    direction = residual + ratio * first[0]
-    image[...] = image[...] + ratio * first[1]
-    last_size = rr_second / reduce_all(6, lane_partial(direction * image[...]))
+    direction = residual + wide_of(ratio) * first[0]
+    product = image[...] + wide_of(ratio) * first[1]
     solution = wide_of(step_size) * first[0] + wide_of(last_size) * direction
-    residual = residual - wide_of(last_size) * image[...]
+    residual = residual - wide_of(last_size) * product
     sub_row = lax.broadcasted_iota(jnp.int32, residual.shape, 1)
     vec[...] = jnp.where(sub_row < 4, solution, residual)
 
@@ -411,26 +434,20 @@
         )
         return carry
 
-    lax.fori_loop(0, leaves, scatter_leaf, 0)
+    lax.fori_loop(0, leaves, scatter_leaf, 0, unroll=4)
     for h in range(leaves):
         tile = acc[h * 8 : h * 8 + 8, :] + acc[leaves * 8 + h * 8 : leaves * 8 + h * 8 + 8, :]
         sol_ref[:, h * LEAF : (h + 1) * LEAF] = tile[:4]
         res_ref[:, h * LEAF : (h + 1) * LEAF] = tile[4:]
 
-    def x_done(j, carry):
-        for copy in x_copies(mine, j, lax.rem(mine + j, spread)):
-            copy.wait_send()
-        return carry
-
-    lax.fori_loop(1, spread, x_done, 0)
+    for part in range(2):
+        for j in far_first(spread):
+            for copy in x_copies(part, mine, j, lax.rem(mine + j, spread)):
+                copy.wait_send()
     for turn in range(ROUNDS):
         me, number = (inner, group) if turn % 2 == 0 else (plane, planes)
-
-        def sent(j, carry):
+        for j in far_first(number):
             tile_copy(turn, me, j, partner(turn, j)[1]).wait_send()
-            return carry
-
-        lax.fori_loop(1, number, sent, 0)
 
 
 def per_device(
@@ -481,8 +498,8 @@
             pltpu.VMEM((2, leaves - 1, ROWS, RANK), f32),
             pltpu.VMEM((ROUNDS, most, ROWS, RANK), f32),
             pltpu.SemaphoreType.DMA((loads,)),
-            pltpu.SemaphoreType.DMA((2, spread - 1)),
-            pltpu.SemaphoreType.DMA((2, spread)),
+            pltpu.SemaphoreType.DMA((4, spread - 1)),
+            pltpu.SemaphoreType.DMA((4, spread)),
             pltpu.SemaphoreType.DMA((ROUNDS, most - 1)),
             pltpu.SemaphoreType.DMA((ROUNDS, most)),
         ],

time: 83.1 us -> 51.8 us (0.62)
  Pallas kernels: 79.1 us -> 47.8 us
    pallas_call x1, Pallas kernels: 79.1 us -> 47.8 us  [per_device(): pl.pallas_call(functools.partial(whole_kernel, (spread, group, planes, le...]
where the time goes in v2:
time: 51.8 us; the launch traced here: 51.6 us
  Pallas kernels  47.8 us (92%)
  local copies, waits for them, and re-layouts  3.14 us (6%)
  between operations  0.64 us (1%)
    pallas_call x1, Pallas kernels, per_device(): pl.pallas_call(functools.partial(whole_kernel, (spread, group, planes, le...  47.8 us
    unnamed x2, local copies, waits for them, and re-layouts  3.14 us

profile of v2, /device:TPU:1, one launch (start us, length us, event | category | flops | bytes accessed | tf_op | source)
XLA Modules:
  0.0 51.6 jit_solution(3489904752121205109)
XLA Ops:
  0.6 47.8 %ridge.1 = (f32[4,8192]{1,0:T(4,128)}, f32[4,8192]{1,0:T(4,128)}) custom-call(f32[4,8192]{1,0:T(4,128)} %tgt_ref.1, f32[8,8192]{1,0:T(8,128)} %pts_ref.1, s32[64,128]{1,0:T(8,128)} %bitcast.5, bf16[32,256,128]{2,1,0:T(8,128)(2,1)} %basis_hbm.1, bf16[31,256,128]{2,1,0:T(8,128)(2,1)} %transfer_hbm.1, bf16[31,128,128]{2,1,0:T(8,128)(2,1)} %coupling_hbm.1, ...), custom_call_target="tpu_custom_call" | custom-call | tf_op jit(solution)/shard_map/ridge/pallas_call | solution.py:476
  48.5 1.6 %copy.12 = f32[4,8192]{1,0:T(4,128)} copy(f32[4,8192]{1,0:T(4,128)} %get-tuple-element.4) | data formatting | bytes 262144
  50.1 1.6 %copy.13 = f32[4,8192]{1,0:T(4,128)} copy(f32[4,8192]{1,0:T(4,128)} %get-tuple-element.5) | data formatting | bytes 262144

commit v3 on v2

--- a/solution.py
+++ b/solution.py
@@ -18,6 +18,7 @@
 bf16 = jnp.bfloat16
 MESH = pl.DeviceIdType.MESH
 ROUNDS = 8
+UNROLL = 8
 
 
 def rounded(values):
@@ -72,6 +73,8 @@
     load_sem,
     x_send,
     x_recv,
+    h_send,
+    h_recv,
     t_send,
     t_recv,
 ):
@@ -135,20 +138,23 @@
     load_basis.start()
     load_transfer.start()
     load_coupling.start()
-    pl.semaphore_wait(barrier, group - 1 + planes - 1 + spread - 1)
-
     low_nodes = group - 1
     parts = (pl.ds(0, low_nodes), pl.ds(low_nodes, nodes - low_nodes))
-
-    def x_copies(part, owner, j, other):
-        own_rows = pl.ds(pl.multiple_of(owner * width, width), width)
+    core = lax.rem(leaf, 2)
+    pair = leaf + 1 - 2 * core
+    half_width = width // 2
+
+    def x_copies(part, owner, half, sems, slot, place):
+        first_row = pl.multiple_of(owner * width + half * half_width, half_width)
+        rows = pl.ds(first_row, half_width)
+        send, recv = sems
         return [
             pltpu.make_async_remote_copy(
-                src_ref=top.at[parts[part], own_rows],
-                dst_ref=top.at[parts[part], own_rows],
-                send_sem=x_send.at[2 * part + k, j - 1],
-                recv_sem=x_recv.at[2 * part + k, owner],
-                device_id=(leaf, other),
+                src_ref=top.at[parts[part], rows],
+                dst_ref=top.at[parts[part], rows],
+                send_sem=send.at[2 * part + k, slot],
+                recv_sem=recv.at[2 * part + k, owner],
+                device_id=place,
                 device_id_type=MESH,
             )
             for k, top in enumerate((top_t, top_c))
@@ -157,18 +163,33 @@
     def far_first(number):
         return sorted(range(1, number), key=lambda j: (-min(j, number - j), j))
 
-    for part in range(2):
-        for copy in top_loads[: 2 * low_levels] if part == 0 else top_loads[2 * low_levels :]:
-            copy.wait()
-        for j in far_first(spread):
-            for copy in x_copies(part, mine, j, lax.rem(mine + j, spread)):
+    across, handed = (x_send, x_recv), (h_send, h_recv)
+
+    def x_start():
+        for part in range(2):
+            for copy in top_loads[: 2 * low_levels] if part == 0 else top_loads[2 * low_levels :]:
+                copy.wait()
+            for j in far_first(spread):
+                place = (leaf, lax.rem(mine + j, spread))
+                for copy in x_copies(part, mine, core, across, j - 1, place):
+                    copy.start()
+
+    def x_hand_over(part):
+        for j in reversed(far_first(spread)):
+            other = lax.rem(mine + j, spread)
+            for copy in x_copies(part, other, core, across, j - 1, (leaf, other)):
+                copy.wait_recv()
+            for copy in x_copies(part, other, core, handed, j - 1, (pair, mine)):
                 copy.start()
 
     def x_wait(part):
-        for j in far_first(spread):
+        for j in reversed(far_first(spread)):
             other = lax.rem(mine + j, spread)
-            for copy in x_copies(part, other, j, other):
+            for copy in x_copies(part, other, 1 - core, handed, j - 1, (pair, mine)):
                 copy.wait_recv()
+
+    pl.semaphore_wait(barrier, group - 1 + planes - 1 + spread - 1)
+    x_start()
 
     def tile_copy(turn, slot, j, other):
         return pltpu.make_async_remote_copy(
@@ -224,12 +245,11 @@
         onehot[c] = hot
         rows_t = jnp.dot(lhs_t[...], hot, preferred_element_type=f32).reshape(leaves, 8, LEAF)
         rows_p = jnp.dot(lhs_p[...], hot, preferred_element_type=f32).reshape(leaves, 16, LEAF)
-        here_t = lax.broadcasted_iota(jnp.int32, (leaves, 8, LEAF), 0) == high[None]
-        here_p = lax.broadcasted_iota(jnp.int32, (leaves, 16, LEAF), 0) == high[None]
-        both = jnp.sum(jnp.where(here_t, rows_t, 0.0), axis=0)
-        spots = jnp.sum(jnp.where(here_p, rows_p, 0.0), axis=0)
+        here = lax.broadcasted_iota(jnp.int32, (leaves, 8, LEAF), 0) == high[None]
+        both = jnp.sum(jnp.where(here, rows_t, 0.0), axis=0)
+        spot_high = jnp.sum(jnp.where(here, rows_p[:, :8], 0.0), axis=0)
+        spot_low = jnp.sum(jnp.where(here, rows_p[:, 8:], 0.0), axis=0)
         vec[c] = both + pltpu.roll(both, 4, 0)
-        spot_high, spot_low = spots[:8], spots[8:]
         whole = spot_high + spot_low
         norm = jnp.sum(whole * whole, axis=0, keepdims=True) * -kernel_rate
         norm_a = rounded(norm)
@@ -257,7 +277,7 @@
         k_low[c] = (values - values_high.astype(f32)).astype(bf16)
         return carry
 
-    lax.fori_loop(0, leaves, gather_leaf, 0, unroll=4)
+    lax.fori_loop(0, leaves, gather_leaf, 0, unroll=min(UNROLL, leaves))
 
     row8 = lax.broadcasted_iota(jnp.int32, (ROWS, RANK), 0)
     upper = row8 < 4
@@ -332,9 +352,11 @@
         exchange_start(turn + 2, jnp.where(upper, inside, extra))
 
         if turn == 0:
-            x_wait(0)
+            x_hand_over(0)
         tiles = exchange_wait(turn)
         group_square = jnp.sum(tiles, axis=0)
+        if turn == 0:
+            x_wait(0)
         levels = [tiles]
         starts = [0]
         place = 0
@@ -353,9 +375,11 @@
         exchange_start(turn + 3, group_sums + jnp.where(upper, 2.0 * inside, 0.0))
 
         if turn == 0:
-            x_wait(1)
+            x_hand_over(1)
         tiles = exchange_wait(turn + 1)
         total_square = jnp.sum(tiles, axis=0)
+        if turn == 0:
+            x_wait(1)
         levels.append(tiles)
         for level in range(high_levels - 1):
             half = levels[-1].shape[0] // 2
@@ -434,7 +458,7 @@
         )
         return carry
 
-    lax.fori_loop(0, leaves, scatter_leaf, 0, unroll=4)
+    lax.fori_loop(0, leaves, scatter_leaf, 0, unroll=min(UNROLL, leaves))
     for h in range(leaves):
         tile = acc[h * 8 : h * 8 + 8, :] + acc[leaves * 8 + h * 8 : leaves * 8 + h * 8 + 8, :]
         sol_ref[:, h * LEAF : (h + 1) * LEAF] = tile[:4]
@@ -442,12 +466,26 @@
 
     for part in range(2):
         for j in far_first(spread):
-            for copy in x_copies(part, mine, j, lax.rem(mine + j, spread)):
+            other = lax.rem(mine + j, spread)
+            for copy in x_copies(part, mine, core, across, j - 1, (leaf, other)):
+                copy.wait_send()
+            for copy in x_copies(part, other, core, handed, j - 1, (pair, mine)):
                 copy.wait_send()
     for turn in range(ROUNDS):
         me, number = (inner, group) if turn % 2 == 0 else (plane, planes)
         for j in far_first(number):
             tile_copy(turn, me, j, partner(turn, j)[1]).wait_send()
+
+
+def hand_out(sol_in, res_in, sol_out, res_out, sem):
+    copies = [
+        pltpu.make_async_copy(sol_in, sol_out, sem.at[0]),
+        pltpu.make_async_copy(res_in, res_out, sem.at[1]),
+    ]
+    for copy in copies:
+        copy.start()
+    for copy in copies:
+        copy.wait()
 
 
 def per_device(
@@ -472,8 +510,9 @@
     most = max(group, planes)
     vmem = pl.BlockSpec(memory_space=pltpu.VMEM)
     any_space = pl.BlockSpec(memory_space=pl.ANY)
+    hbm_space = pl.BlockSpec(memory_space=pltpu.HBM)
     out = jax.ShapeDtypeStruct((columns, here), f32)
-    return pl.pallas_call(
+    results = pl.pallas_call(
         functools.partial(whole_kernel, (spread, group, planes, leaves)),
         out_shape=(out, out),
         in_specs=[vmem, vmem, vmem] + [any_space] * 5,
@@ -500,6 +539,8 @@
             pltpu.SemaphoreType.DMA((loads,)),
             pltpu.SemaphoreType.DMA((4, spread - 1)),
             pltpu.SemaphoreType.DMA((4, spread)),
+            pltpu.SemaphoreType.DMA((4, spread - 1)),
+            pltpu.SemaphoreType.DMA((4, spread)),
             pltpu.SemaphoreType.DMA((ROUNDS, most - 1)),
             pltpu.SemaphoreType.DMA((ROUNDS, most)),
         ],
@@ -517,6 +558,14 @@
         transfer_top.transpose(0, 2, 1),
         coupling_top.transpose(0, 2, 1),
     )
+    return pl.pallas_call(
+        hand_out,
+        out_shape=(out, out),
+        in_specs=[vmem, vmem],
+        out_specs=(hbm_space, hbm_space),
+        scratch_shapes=[pltpu.SemaphoreType.DMA((2,))],
+        name="hand_out",
+    )(*results)
 
 
 def solution(mesh):

time: 51.8 us -> 48.6 us (0.938)
  local copies, waits for them, and re-layouts: 3.14 us -> 0 us
    unnamed x2 -> x0, local copies, waits for them, and re-layouts: 3.14 us -> none
    pallas_call x1, Pallas kernels: 47.8 us -> 46.1 us  [per_device(): pl.pallas_call(functools.partial(whole_kernel, (spread, group, planes, le...]
    pallas_call x0 -> x1, Pallas kernels: none -> 1.68 us  [per_device(): pl.pallas_call(hand_out, out_shape=(out, out), in_specs=[vmem, vmem], out...]
where the time goes in v3:
time: 48.6 us; the launch traced here: 48.4 us
  Pallas kernels  47.8 us (98%)
  between operations  0.64 us (1%)
    pallas_call x1, Pallas kernels, per_device(): pl.pallas_call(functools.partial(whole_kernel, (spread, group, planes, le...  46.1 us
    pallas_call x1, Pallas kernels, per_device(): pl.pallas_call(hand_out, out_shape=(out, out), in_specs=[vmem, vmem], out...  1.68 us

profile of v3, /device:TPU:1, one launch (start us, length us, event | category | flops | bytes accessed | tf_op | source)
XLA Modules:
  0.0 48.4 jit_solution(9214116315971072522)
XLA Ops:
  0.6 46.1 %ridge.1 = (f32[4,8192]{1,0:T(4,128)}, f32[4,8192]{1,0:T(4,128)}) custom-call(f32[4,8192]{1,0:T(4,128)} %tgt_ref.1, f32[8,8192]{1,0:T(8,128)} %pts_ref.1, s32[64,128]{1,0:T(8,128)} %bitcast.5, bf16[32,256,128]{2,1,0:T(8,128)(2,1)} %basis_hbm.1, bf16[31,256,128]{2,1,0:T(8,128)(2,1)} %transfer_hbm.1, bf16[31,128,128]{2,1,0:T(8,128)(2,1)} %coupling_hbm.1, ...), custom_call_target="tpu_custom_call" | custom-call | tf_op jit(solution)/shard_map/ridge/pallas_call | solution.py:515
  46.8 1.7 %hand_out.1 = (f32[4,8192]{1,0:T(4,128)}, f32[4,8192]{1,0:T(4,128)}) custom-call(f32[4,8192]{1,0:T(4,128)} %get-tuple-element.4.sol_in, f32[4,8192]{1,0:T(4,128)} %get-tuple-element.5.res_in), custom_call_target="tpu_custom_call" | custom-call | tf_op jit(solution)/shard_map/hand_out/pallas_call | solution.py:561

commit v4 on v3

--- a/solution.py
+++ b/solution.py
@@ -277,7 +277,7 @@
         k_low[c] = (values - values_high.astype(f32)).astype(bf16)
         return carry
 
-    lax.fori_loop(0, leaves, gather_leaf, 0, unroll=min(UNROLL, leaves))
+    lax.fori_loop(0, leaves, gather_leaf, 0, unroll=min(2 * UNROLL, leaves))
 
     row8 = lax.broadcasted_iota(jnp.int32, (ROWS, RANK), 0)
     upper = row8 < 4
@@ -320,6 +320,29 @@
         toward = batched(paired[:, 1].astype(bf16), top_c[place : place + half])
         return jnp.sum(paired[:, 0] * toward, axis=0)
 
+    def scatter(source, k):
+        sub_row = lax.broadcasted_iota(jnp.int32, (ROWS, LEAF), 0)
+        inner_steps = min(UNROLL, leaves)
+
+        def step(i, carry):
+            total = jnp.zeros((leaves * 8, LEAF), f32)
+            for t in range(inner_steps):
+                c = i * inner_steps + t
+                high = lax.shift_right_logical(index_row(c), 8)
+                here = lax.broadcasted_iota(jnp.int32, (leaves, 8, LEAF), 0) == high[None]
+                value = source[c]
+                value_high = rounded(value)
+                pieces = jnp.where(sub_row < 4, value_high, value - value_high)
+                rows = jnp.where(here, pieces[None], 0.0).reshape(leaves * 8, LEAF).astype(bf16)
+                total = total + lax.dot_general(
+                    rows, onehot[c], (((1,), (1,)), ((), ())), preferred_element_type=f32
+                )
+            acc[k] += total
+            return carry
+
+        acc[k] = jnp.zeros((leaves * 8, LEAF), f32)
+        lax.fori_loop(0, leaves // inner_steps, step, 0)
+
     def apply_matrix(turn, extra):
         value = vec[...]
         square = lane_partial(value * value)
@@ -371,6 +394,8 @@
         inside = jnp.zeros((ROWS, RANK), f32)
         for level in range(low_levels):
             inside = inside + level_product(levels[level], starts[level])
+        if turn > 0:
+            scatter(first, 0)
         group_sums = jnp.sum(exchange_wait(turn + 2), axis=0)
         exchange_start(turn + 3, group_sums + jnp.where(upper, 2.0 * inside, 0.0))
 
@@ -404,6 +429,8 @@
             right = child[:, :, RANK:] + links[1, offset : offset + half]
             field = jnp.stack([left, right], axis=1).reshape(2 * half, ROWS, RANK)
         image[...] = dense[...] + batched_t(field.astype(bf16), basis[...])
+        if turn > 0:
+            scatter(image, 1)
 
         inside = jnp.zeros((ROWS, RANK), f32)
         for level in range(low_levels, low_levels + high_levels):
@@ -425,44 +452,28 @@
     step_size = rr_first / curve_first
     start = vec[...]
     product = image[...]
-    first[0] = start
-    first[1] = product
+    first[...] = product
     residual = start - wide_of(step_size) * product
     vec[...] = residual
 
     rr_second, curve, cross = apply_matrix(4, lane_partial(residual * product))
     ratio = rr_second / rr_first
     last_size = rr_second / (curve + 2.0 * ratio * cross + ratio * ratio * curve_first)
-    residual = vec[...]
-    direction = residual + wide_of(ratio) * first[0]
-    product = image[...] + wide_of(ratio) * first[1]
-    solution = wide_of(step_size) * first[0] + wide_of(last_size) * direction
-    residual = residual - wide_of(last_size) * product
-    sub_row = lax.broadcasted_iota(jnp.int32, residual.shape, 1)
-    vec[...] = jnp.where(sub_row < 4, solution, residual)
-
-    acc[...] = jnp.zeros_like(acc)
-
-    def scatter_leaf(c, carry):
-        order = index_row(c)
-        high = lax.shift_right_logical(order, 8)
-        here = lax.broadcasted_iota(jnp.int32, (leaves, 8, LEAF), 0) == high[None]
-        value = vec[c]
-        value_high = rounded(value)
-        value_low = value - value_high
-        part_high = jnp.where(here, value_high[None], 0.0).reshape(leaves * 8, LEAF)
-        part_low = jnp.where(here, value_low[None], 0.0).reshape(leaves * 8, LEAF)
-        rows = jnp.concatenate([part_high, part_low], axis=0).astype(bf16)
-        acc[...] += lax.dot_general(
-            rows, onehot[c], (((1,), (1,)), ((), ())), preferred_element_type=f32
-        )
-        return carry
-
-    lax.fori_loop(0, leaves, scatter_leaf, 0, unroll=min(UNROLL, leaves))
+    step_size, ratio, last_size = (
+        jnp.concatenate([tile, tile], axis=1)[:4] for tile in (step_size, ratio, last_size)
+    )
+
     for h in range(leaves):
-        tile = acc[h * 8 : h * 8 + 8, :] + acc[leaves * 8 + h * 8 : leaves * 8 + h * 8 + 8, :]
-        sol_ref[:, h * LEAF : (h + 1) * LEAF] = tile[:4]
-        res_ref[:, h * LEAF : (h + 1) * LEAF] = tile[4:]
+        tile = acc[0, h * 8 : h * 8 + 8, :]
+        image_first = (tile + swap(tile))[:4]
+        tile = acc[1, h * 8 : h * 8 + 8, :]
+        image_second = (tile + swap(tile))[:4]
+        start = tgt_ref[:, h * LEAF : (h + 1) * LEAF]
+        residual = start - step_size * image_first
+        direction = residual + ratio * start
+        sol_ref[:, h * LEAF : (h + 1) * LEAF] = step_size * start + last_size * direction
+        product = image_second + ratio * image_first
+        res_ref[:, h * LEAF : (h + 1) * LEAF] = residual - last_size * product
 
     for part in range(2):
         for j in far_first(spread):
@@ -532,8 +543,8 @@
             pltpu.VMEM((leaves, ROWS, LEAF), f32),
             pltpu.VMEM((leaves, ROWS, LEAF), f32),
             pltpu.VMEM((leaves, ROWS, LEAF), f32),
-            pltpu.VMEM((2, leaves, ROWS, LEAF), f32),
-            pltpu.VMEM((2 * leaves * 8, LEAF), f32),
+            pltpu.VMEM((leaves, ROWS, LEAF), f32),
+            pltpu.VMEM((2, leaves * 8, LEAF), f32),
             pltpu.VMEM((2, leaves - 1, ROWS, RANK), f32),
             pltpu.VMEM((ROUNDS, most, ROWS, RANK), f32),
             pltpu.SemaphoreType.DMA((loads,)),

time: 48.6 us -> 46.9 us (0.965)
  Pallas kernels: 47.8 us -> 46.1 us
    pallas_call x1, Pallas kernels: 46.1 us -> 44.5 us  [per_device(): pl.pallas_call(functools.partial(whole_kernel, (spread, group, planes, le...]
where the time goes in v4:
time: 46.9 us; the launch traced here: 46.8 us
  Pallas kernels  46.1 us (98%)
  between operations  0.64 us (1%)
    pallas_call x1, Pallas kernels, per_device(): pl.pallas_call(functools.partial(whole_kernel, (spread, group, planes, le...  44.5 us
    pallas_call x1, Pallas kernels, per_device(): pl.pallas_call(hand_out, out_shape=(out, out), in_specs=[vmem, vmem], out...  1.68 us

profile of v4, /device:TPU:1, one launch (start us, length us, event | category | flops | bytes accessed | tf_op | source)
XLA Modules:
  0.0 46.8 jit_solution(11727287509587062875)
XLA Ops:
  0.6 44.5 %ridge.1 = (f32[4,8192]{1,0:T(4,128)}, f32[4,8192]{1,0:T(4,128)}) custom-call(f32[4,8192]{1,0:T(4,128)} %tgt_ref.1, f32[8,8192]{1,0:T(8,128)} %pts_ref.1, s32[64,128]{1,0:T(8,128)} %bitcast.5, bf16[32,256,128]{2,1,0:T(8,128)(2,1)} %basis_hbm.1, bf16[31,256,128]{2,1,0:T(8,128)(2,1)} %transfer_hbm.1, bf16[31,128,128]{2,1,0:T(8,128)(2,1)} %coupling_hbm.1, ...), custom_call_target="tpu_custom_call" | custom-call | tf_op jit(solution)/shard_map/ridge/pallas_call | solution.py:526
  45.1 1.7 %hand_out.1 = (f32[4,8192]{1,0:T(4,128)}, f32[4,8192]{1,0:T(4,128)}) custom-call(f32[4,8192]{1,0:T(4,128)} %get-tuple-element.4.sol_in, f32[4,8192]{1,0:T(4,128)} %get-tuple-element.5.res_in), custom_call_target="tpu_custom_call" | custom-call | tf_op jit(solution)/shard_map/hand_out/pallas_call | solution.py:572

commit v5 on v4

--- a/solution.py
+++ b/solution.py
@@ -77,6 +77,8 @@
     h_recv,
     t_send,
     t_recv,
+    basis_t,
+    transfer_t,
 ):
     spread, group, planes, leaves = sizes
     leaf = lax.axis_index("leaf")
@@ -101,10 +103,6 @@
         other = lax.rem(mine + j, spread)
         pl.semaphore_signal(barrier, inc=1, device_id=(leaf, other), device_id_type=MESH)
         return carry
-
-    lax.fori_loop(1, group, greet_inner, 0)
-    lax.fori_loop(1, planes, greet_plane, 0)
-    lax.fori_loop(1, spread, greet_x, 0)
 
     width = RANK // spread
     mine_rows = pl.ds(pl.multiple_of(mine * width, width), width)
@@ -138,6 +136,21 @@
     load_basis.start()
     load_transfer.start()
     load_coupling.start()
+
+    lax.fori_loop(1, group, greet_inner, 0)
+    lax.fori_loop(1, planes, greet_plane, 0)
+    lax.fori_loop(1, spread, greet_x, 0)
+
+    for h in range(leaves):
+        piece = tgt_ref[:, h * LEAF : (h + 1) * LEAF]
+        high = rounded(piece)
+        lhs_t32[h * 8 : h * 8 + 4, :] = high
+        lhs_t32[h * 8 + 4 : h * 8 + 8, :] = piece - high
+        piece = pts_ref[:, h * LEAF : (h + 1) * LEAF]
+        high = rounded(piece)
+        lhs_p[h * 16 : (h + 1) * 16, :] = jnp.concatenate([high, piece - high], axis=0).astype(bf16)
+    lhs_t[...] = lhs_t32[...].astype(bf16)
+
     low_nodes = group - 1
     parts = (pl.ds(0, low_nodes), pl.ds(low_nodes, nodes - low_nodes))
     core = lax.rem(leaf, 2)
@@ -220,16 +233,6 @@
             slot, other = partner(turn, j)
             tile_copy(turn, slot, j, other).wait_recv()
         return slots[turn, :number]
-
-    for h in range(leaves):
-        piece = tgt_ref[:, h * LEAF : (h + 1) * LEAF]
-        high = rounded(piece)
-        lhs_t32[h * 8 : h * 8 + 4, :] = high
-        lhs_t32[h * 8 + 4 : h * 8 + 8, :] = piece - high
-        piece = pts_ref[:, h * LEAF : (h + 1) * LEAF]
-        high = rounded(piece)
-        lhs_p[h * 16 : (h + 1) * 16, :] = jnp.concatenate([high, piece - high], axis=0).astype(bf16)
-    lhs_t[...] = lhs_t32[...].astype(bf16)
 
     def index_row(c):
         return jnp.concatenate(
@@ -322,7 +325,7 @@
 
     def scatter(source, k):
         sub_row = lax.broadcasted_iota(jnp.int32, (ROWS, LEAF), 0)
-        inner_steps = min(UNROLL, leaves)
+        inner_steps = min(2 * UNROLL, leaves)
 
         def step(i, carry):
             total = jnp.zeros((leaves * 8, LEAF), f32)
@@ -400,6 +403,12 @@
         exchange_start(turn + 3, group_sums + jnp.where(upper, 2.0 * inside, 0.0))
 
         if turn == 0:
+            def turn_round(c, carry):
+                basis_t[c] = basis[c].T
+                transfer_t[lax.rem(c, leaves - 1)] = transfer[lax.rem(c, leaves - 1)].T
+                return carry
+
+            lax.fori_loop(0, leaves, turn_round, 0, unroll=min(UNROLL, leaves))
             x_hand_over(1)
         tiles = exchange_wait(turn + 1)
         total_square = jnp.sum(tiles, axis=0)
@@ -424,11 +433,11 @@
         field = both_halves(field)[None]
 
         for _, offset, half in reversed(saved):
-            child = batched_t(field.astype(bf16), transfer[offset : offset + half])
+            child = batched(field.astype(bf16), transfer_t[offset : offset + half])
             left = child[:, :, :RANK] + links[0, offset : offset + half]
             right = child[:, :, RANK:] + links[1, offset : offset + half]
             field = jnp.stack([left, right], axis=1).reshape(2 * half, ROWS, RANK)
-        image[...] = dense[...] + batched_t(field.astype(bf16), basis[...])
+        image[...] = dense[...] + batched(field.astype(bf16), basis_t[...])
         if turn > 0:
             scatter(image, 1)
 
@@ -554,6 +563,8 @@
             pltpu.SemaphoreType.DMA((4, spread)),
             pltpu.SemaphoreType.DMA((ROUNDS, most - 1)),
             pltpu.SemaphoreType.DMA((ROUNDS, most)),
+            pltpu.VMEM((leaves, RANK, LEAF), bf16),
+            pltpu.VMEM((leaves - 1, RANK, 2 * RANK), bf16),
         ],
         compiler_params=pltpu.CompilerParams(
             collective_id=0, has_side_effects=True, vmem_limit_bytes=56 * 1024 * 1024

time: 46.9 us -> 45.7 us (0.974)
  Pallas kernels: 46.1 us -> 44.9 us
    pallas_call x1, Pallas kernels: 44.5 us -> 43.2 us  [per_device(): pl.pallas_call(functools.partial(whole_kernel, (spread, group, planes, le...]
where the time goes in v5:
time: 45.7 us; the launch traced here: 45.6 us
  Pallas kernels  44.9 us (98%)
  between operations  0.64 us (1%)
    pallas_call x1, Pallas kernels, per_device(): pl.pallas_call(functools.partial(whole_kernel, (spread, group, planes, le...  43.2 us
    pallas_call x1, Pallas kernels, per_device(): pl.pallas_call(hand_out, out_shape=(out, out), in_specs=[vmem, vmem], out...  1.68 us

profile of v5, /device:TPU:1, one launch (start us, length us, event | category | flops | bytes accessed | tf_op | source)
XLA Modules:
  0.0 45.6 jit_solution(12893701737876379236)
XLA Ops:
  0.6 43.2 %ridge.1 = (f32[4,8192]{1,0:T(4,128)}, f32[4,8192]{1,0:T(4,128)}) custom-call(f32[4,8192]{1,0:T(4,128)} %tgt_ref.1, f32[8,8192]{1,0:T(8,128)} %pts_ref.1, s32[64,128]{1,0:T(8,128)} %bitcast.5, bf16[32,256,128]{2,1,0:T(8,128)(2,1)} %basis_hbm.1, bf16[31,256,128]{2,1,0:T(8,128)(2,1)} %transfer_hbm.1, bf16[31,128,128]{2,1,0:T(8,128)(2,1)} %coupling_hbm.1, ...), custom_call_target="tpu_custom_call" | custom-call | tf_op jit(solution)/shard_map/ridge/pallas_call | solution.py:535
  43.9 1.7 %hand_out.1 = (f32[4,8192]{1,0:T(4,128)}, f32[4,8192]{1,0:T(4,128)}) custom-call(f32[4,8192]{1,0:T(4,128)} %get-tuple-element.4.sol_in, f32[4,8192]{1,0:T(4,128)} %get-tuple-element.5.res_in), custom_call_target="tpu_custom_call" | custom-call | tf_op jit(solution)/shard_map/hand_out/pallas_call | solution.py:583

commit v6 on v5

--- a/solution.py
+++ b/solution.py
@@ -423,6 +423,10 @@
         for level in range(low_levels, low_levels + high_levels):
             owns.append(level_links(level, levels[level], starts[level]))
 
+        inside = jnp.zeros((ROWS, RANK), f32)
+        for level in range(low_levels, low_levels + high_levels):
+            inside = inside + level_product(levels[level], starts[level])
+
         field = None
         for own, side, node in reversed(owns):
             if field is not None:
@@ -441,9 +445,6 @@
         if turn > 0:
             scatter(image, 1)
 
-        inside = jnp.zeros((ROWS, RANK), f32)
-        for level in range(low_levels, low_levels + high_levels):
-            inside = inside + level_product(levels[level], starts[level])
         sums = jnp.sum(exchange_wait(turn + 3), axis=0)
         sums = full(sums + jnp.where(upper, 2.0 * inside, 0.0))
         total_square = full(total_square)

time: 45.7 us -> 45.5 us (level)
  no operation moved by 1% of the time
where the time goes in v6:
time: 45.5 us; the launch traced here: 45.3 us
  Pallas kernels  44.7 us (98%)
  between operations  0.64 us (1%)
    pallas_call x1, Pallas kernels, per_device(): pl.pallas_call(functools.partial(whole_kernel, (spread, group, planes, le...  43 us
    pallas_call x1, Pallas kernels, per_device(): pl.pallas_call(hand_out, out_shape=(out, out), in_specs=[vmem, vmem], out...  1.68 us

profile of v6, /device:TPU:1, one launch (start us, length us, event | category | flops | bytes accessed | tf_op | source)
XLA Modules:
  0.0 45.3 jit_solution(12724723031571761829)
XLA Ops:
  0.6 43.0 %ridge.1 = (f32[4,8192]{1,0:T(4,128)}, f32[4,8192]{1,0:T(4,128)}) custom-call(f32[4,8192]{1,0:T(4,128)} %tgt_ref.1, f32[8,8192]{1,0:T(8,128)} %pts_ref.1, s32[64,128]{1,0:T(8,128)} %bitcast.5, bf16[32,256,128]{2,1,0:T(8,128)(2,1)} %basis_hbm.1, bf16[31,256,128]{2,1,0:T(8,128)(2,1)} %transfer_hbm.1, bf16[31,128,128]{2,1,0:T(8,128)(2,1)} %coupling_hbm.1, ...), custom_call_target="tpu_custom_call" | custom-call | tf_op jit(solution)/shard_map/ridge/pallas_call | solution.py:536
  43.7 1.7 %hand_out.1 = (f32[4,8192]{1,0:T(4,128)}, f32[4,8192]{1,0:T(4,128)}) custom-call(f32[4,8192]{1,0:T(4,128)} %get-tuple-element.4.sol_in, f32[4,8192]{1,0:T(4,128)} %get-tuple-element.5.res_in), custom_call_target="tpu_custom_call" | custom-call | tf_op jit(solution)/shard_map/hand_out/pallas_call | solution.py:584

commit v7 on v6

--- a/solution.py
+++ b/solution.py
@@ -498,14 +498,21 @@
             tile_copy(turn, me, j, partner(turn, j)[1]).wait_send()
 
 
-def hand_out(sol_in, res_in, sol_out, res_out, sem):
-    copies = [
-        pltpu.make_async_copy(sol_in, sol_out, sem.at[0]),
-        pltpu.make_async_copy(res_in, res_out, sem.at[1]),
+def hand_out(sol_in, res_in, sol_out, res_out, held, sem):
+    arrive = [
+        pltpu.make_async_copy(source, held.at[k], sem.at[k])
+        for k, source in enumerate((sol_in, res_in))
     ]
-    for copy in copies:
+    leave = [
+        pltpu.make_async_copy(held.at[k], target, sem.at[2 + k])
+        for k, target in enumerate((sol_out, res_out))
+    ]
+    for copy in arrive:
         copy.start()
-    for copy in copies:
+    for before, after in zip(arrive, leave):
+        before.wait()
+        after.start()
+    for copy in leave:
         copy.wait()
 
 
@@ -584,9 +591,9 @@
     return pl.pallas_call(
         hand_out,
         out_shape=(out, out),
-        in_specs=[vmem, vmem],
+        in_specs=[hbm_space, hbm_space],
         out_specs=(hbm_space, hbm_space),
-        scratch_shapes=[pltpu.SemaphoreType.DMA((2,))],
+        scratch_shapes=[pltpu.VMEM((2, columns, here), f32), pltpu.SemaphoreType.DMA((4,))],
         name="hand_out",
     )(*results)
 

time: 45.5 us -> 45.4 us (level)
  no operation moved by 1% of the time
where the time goes in v7:
time: 45.4 us; the launch traced here: 45.3 us
  Pallas kernels  44.7 us (98%)
  between operations  0.64 us (1%)
    pallas_call x1, Pallas kernels, per_device(): pl.pallas_call(functools.partial(whole_kernel, (spread, group, planes, le...  43 us
    pallas_call x1, Pallas kernels, per_device(): pl.pallas_call(hand_out, out_shape=(out, out), in_specs=[hbm_space, hbm_s...  1.66 us

profile of v7, /device:TPU:1, one launch (start us, length us, event | category | flops | bytes accessed | tf_op | source)
XLA Modules:
  0.0 45.3 jit_solution(145159213581987038)
XLA Ops:
  0.6 43.0 %ridge.1 = (f32[4,8192]{1,0:T(4,128)}, f32[4,8192]{1,0:T(4,128)}) custom-call(f32[4,8192]{1,0:T(4,128)} %tgt_ref.1, f32[8,8192]{1,0:T(8,128)} %pts_ref.1, s32[64,128]{1,0:T(8,128)} %bitcast.5, bf16[32,256,128]{2,1,0:T(8,128)(2,1)} %basis_hbm.1, bf16[31,256,128]{2,1,0:T(8,128)(2,1)} %transfer_hbm.1, bf16[31,128,128]{2,1,0:T(8,128)(2,1)} %coupling_hbm.1, ...), custom_call_target="tpu_custom_call" | custom-call | tf_op jit(solution)/shard_map/ridge/pallas_call | solution.py:543
  43.7 1.7 %hand_out.1 = (f32[4,8192]{1,0:T(4,128)}, f32[4,8192]{1,0:T(4,128)}) custom-call(f32[4,8192]{1,0:T(4,128)} %get-tuple-element.4.sol_in, f32[4,8192]{1,0:T(4,128)} %get-tuple-element.5.res_in), custom_call_target="tpu_custom_call" | custom-call | tf_op jit(solution)/shard_map/hand_out/pallas_call | solution.py:591
